TPU v7x, 32 devices: a whole 2x2x4 slice. The times are simulated.
32 devices in a mesh: tm: 4 (over y, x), nrn: 8 (over z, core).
Axes of the slice: x: 2, y: 2, z: 4, core: 2. Of those that a mesh axis runs over, the one named last changes fastest.
Arguments:
- spikes: bfloat16 [8192, 32768], P('tm', 'nrn'), may hold values from -6 to 6
- read_in: bfloat16 [32768, 128], P('nrn'), may hold values from -0.03125 to 0.03125
- kernel: float32 [128, 8192], P(('tm', 'nrn')), may hold values from -0.0625 to 0.0625
- gain: float32 [128], replicated, may hold values from 0.1 to 1.9
- w_gate: bfloat16 [128, 512], replicated, may hold values from -0.5 to 0.5
- w_up: bfloat16 [128, 512], replicated, may hold values from -0.5 to 0.5
- w_down: bfloat16 [512, 128], replicated, may hold values from -0.25 to 0.25
Outputs:
- denoised: bfloat16 [8192, 128], P(('tm', 'nrn'))
All inputs are finite; a program needn't handle non-finite values.
Results may differ from a plain program's by a relative error of at most 0.0045.
Values sent between devices are 32-bit elements; how exact they have to be, the bound alone decides.
A program may use at most 64 MiB of HBM per device.

v0:
```python
import math

import jax
import jax.numpy as jnp
from jax import lax
from jax.sharding import PartitionSpec as P

precise = lax.Precision.HIGHEST


def dft_table(order):
    index = jnp.arange(order, dtype=jnp.int32)
    phase = index[:, None] * index[None, :] % order
    angles = phase.astype(jnp.float32) * (2.0 * math.pi / order)
    return (jnp.cos(angles), jnp.sin(angles))


def twiddle_table(outer, inner):
    outer_index = jnp.arange(outer, dtype=jnp.int32)
    inner_index = jnp.arange(inner, dtype=jnp.int32)
    phase = outer_index[:, None] * inner_index[None, :] % (outer * inner)
    angles = phase.astype(jnp.float32) * (2.0 * math.pi / (outer * inner))
    return (jnp.cos(angles), jnp.sin(angles))


def forward_dft(signal, tables):
    cos_outer, sin_outer, cos_twist, sin_twist, cos_inner, sin_inner = tables
    real_part = jnp.einsum("ar,crs->cas", cos_outer, signal, precision=precise)
    imag_part = -jnp.einsum("ar,crs->cas", sin_outer, signal, precision=precise)
    twist_real = real_part * cos_twist + imag_part * sin_twist
    twist_imag = imag_part * cos_twist - real_part * sin_twist
    spec_real = jnp.einsum("cas,sb->cab", twist_real, cos_inner, precision=precise) + jnp.einsum(
        "cas,sb->cab", twist_imag, sin_inner, precision=precise
    )
    spec_imag = jnp.einsum("cas,sb->cab", twist_imag, cos_inner, precision=precise) - jnp.einsum(
        "cas,sb->cab", twist_real, sin_inner, precision=precise
    )
    return (spec_real, spec_imag)


def inverse_dft(spec_real, spec_imag, tables):
    cos_outer, sin_outer, cos_twist, sin_twist, cos_inner, sin_inner = tables
    back_real = jnp.einsum("cab,bs->cas", spec_real, cos_inner, precision=precise) - jnp.einsum(
        "cab,bs->cas", spec_imag, sin_inner, precision=precise
    )
    back_imag = jnp.einsum("cab,bs->cas", spec_real, sin_inner, precision=precise) + jnp.einsum(
        "cab,bs->cas", spec_imag, cos_inner, precision=precise
    )
    turn_real = back_real * cos_twist - back_imag * sin_twist
    turn_imag = back_real * sin_twist + back_imag * cos_twist
    result = jnp.einsum("ra,cas->crs", cos_outer, turn_real, precision=precise) - jnp.einsum(
        "ra,cas->crs", sin_outer, turn_imag, precision=precise
    )
    return result / (cos_outer.shape[0] * cos_inner.shape[0])


def per_device(spikes, read_in, kernel, gain, w_gate, w_up, w_down):
    time_groups = lax.axis_size("tm")
    neuron_groups = lax.axis_size("nrn")
    devices = time_groups * neuron_groups
    tok_rows = spikes.shape[0] // neuron_groups
    latent_width = read_in.shape[1]
    channels_dev = latent_width // devices
    session = tok_rows * devices
    latent = lax.psum_scatter(
        jnp.dot(spikes, read_in, preferred_element_type=jnp.float32),
        "nrn",
        scatter_dimension=0,
        tiled=True,
    )
    flipped = latent.T
    series = lax.all_to_all(flipped, ("tm", "nrn"), split_axis=0, concat_axis=1, tiled=True)
    cos_outer, sin_outer = dft_table(devices)
    cos_inner, sin_inner = dft_table(tok_rows)
    cos_twist, sin_twist = twiddle_table(devices, tok_rows)
    tables = (cos_outer, sin_outer, cos_twist, sin_twist, cos_inner, sin_inner)
    data_real, data_imag = forward_dft(series.reshape(channels_dev, devices, tok_rows), tables)
    kern_real, kern_imag = forward_dft(kernel.reshape(channels_dev, devices, tok_rows), tables)
    prod_real = data_real * kern_real - data_imag * kern_imag
    prod_imag = data_real * kern_imag + data_imag * kern_real
    conv = inverse_dft(prod_real, prod_imag, tables).reshape(channels_dev, session)
    mixed = series + conv
    stacked = lax.all_to_all(mixed, ("tm", "nrn"), split_axis=1, concat_axis=0, tiled=True)
    residual = stacked.T
    meansq = jnp.mean(residual * residual, axis=-1, keepdims=True)
    normed = (residual * lax.rsqrt(meansq + 1e-05) * gain).astype(jnp.bfloat16)
    gate = jnp.dot(normed, w_gate, preferred_element_type=jnp.float32)
    upper = jnp.dot(normed, w_up, preferred_element_type=jnp.float32)
    act = (jax.nn.silu(gate) * upper).astype(jnp.bfloat16)
    return (residual + jnp.dot(act, w_down, preferred_element_type=jnp.float32)).astype(
        jnp.bfloat16
    )


def solution(mesh):
    placed = (P("tm", "nrn"), P("nrn", None), P(("tm", "nrn"), None), P(), P(), P(), P())
    return jax.shard_map(
        per_device, mesh=mesh, in_specs=placed, out_specs=P(("tm", "nrn"), None), check_vma=False
    )
```

profile of v0, /device:TPU:0, one launch (start us, length us, event | category | flops | bytes accessed | tf_op | source)
XLA Modules:
  0.0 94.9 jit_solution(12043819451958355884)
XLA Ops:
  6.5 0.0 copy-start
  6.5 0.0 copy-start.1
  6.5 0.0 copy-start.3
  6.5 0.0 copy-start.2
  6.5 0.0 copy-start.5
  6.5 0.0 copy-start.4
  6.6 0.0 reduce-scatter.2.cloned.1.call-start
  6.6 1.2 %copy-done = bf16[4096,128]{1,0:T(8,128)(2,1)S(1)} copy-done((bf16[4096,128]{1,0:T(8,128)(2,1)S(1)}, bf16[4096,128]{1,0:T(8,128)(2,1)}, u32[]{:S(2)}) %copy-start) | copy-done | bytes 1048600
  7.8 9.1 %fusion.190 = f32[2048,128]{1,0:T(8,128)} fusion(bf16[2048,4096]{1,0:T(8,128)(2,1)} %param.7, bf16[4096,128]{1,0:T(8,128)(2,1)S(1)} %copy-done), kind=kOutput, calls=%fused_computation.196 | convolution fusion | flops 2147483648 | bytes 18874368 | tf_op jit(solution)/shard_map/dot_general | solution.py:66
  16.8 0.0 reduce-scatter.2.cloned.1.call-update
  16.9 0.1 fusion.104
  17.0 0.0 copy-done.1
  17.0 0.4 convolution_negate_fusion
  17.4 0.3 fusion.39
  17.7 1.3 %fusion.26 = f32[4,32,256]{2,1,0:T(8,128)S(1)} fusion(f32[32,4,256]{2,0,1:T(8,128)S(1)} %fusion.39, f32[32,4,256]{2,0,1:T(8,128)S(1)} %convolution_negate_fusion, f32[32,256]{1,0:T(8,128)S(1)} %get-tuple-element.7, f32[32,256]{1,0:T(8,128)S(1)} %get-tuple-element.8), kind=kOutput, calls=%fused_computation.40 | convolution fusion | flops 101679104 | bytes 458752 | tf_op jit(solution)/shard_map/cas,sb->cab/dot_general | solution.py:35
  19.0 1.3 %convolution_subtract_fusion.1 = f32[4,32,256]{2,1,0:T(8,128)S(1)} fusion(f32[4,32,256]{2,1,0:T(8,128)S(1)} %fusion.26, f32[32,4,256]{2,0,1:T(8,128)S(1)} %convolution_negate_fusion, f32[32,4,256]{2,0,1:T(8,128)S(1)} %fusion.39, f32[32,256]{1,0:T(8,128)S(1)} %get-tuple-element.7, f32[32,256]{1,0:T(8,128)S(1)} %get-tuple-element.8), kind=kOutput, calls=%fused_computation.6 | convolution fusion | flops 101711872 | bytes 589824 | tf_op jit(solution)/shard_map/cas,sb->cab/dot_general | solution.py:35
  20.3 31.8 %reduce-scatter.2.cloned.1.call-done = f32[256,128]{1,0:T(8,128)} async-done(((f32[2048,128]{1,0:T(8,128)}), f32[256,128]{1,0:T(8,128)}) %reduce-scatter.2.cloned.1.call-update) | async-done | bytes 131088 | tf_op jit(solution)/shard_map/reduce_scatter | solution.py:65
  52.1 1.0 %copy.13 = f32[128,256]{1,0:T(8,128)S(1)} copy(f32[128,256]{0,1:T(8,128)} %bitcast.99) | data formatting | bytes 262144 | tf_op jit(solution)/shard_map/transpose | solution.py:71
  53.1 0.7 all_to_all.24
  53.8 3.0 %all-to-all-start = ((f32[32,4,256]{2,1,0:T(4,128)}), f32[32,4,256]{2,1,0:T(4,128)S(1)}, u32[]{:S(2)}, u32[]{:S(2)}) async-start(f32[32,4,256]{2,1,0:T(4,128)} %all_to_all.24), calls=%async_computation.1 | async-start | bytes 262144 | tf_op jit(solution)/shard_map/all_to_all | solution.py:72
  56.9 1.3 %fusion.30 = f32[4,32,256]{2,1,0:T(8,128)S(1)} fusion(f32[32,4,256]{2,0,1:T(8,128)S(1)} %convolution_negate_fusion, f32[32,4,256]{2,0,1:T(8,128)S(1)} %fusion.39, f32[32,256]{1,0:T(8,128)S(1)} %get-tuple-element.7, f32[32,256]{1,0:T(8,128)S(1)} %get-tuple-element.8), kind=kOutput, calls=%fused_computation.44 | convolution fusion | flops 101679104 | bytes 458752 | tf_op jit(solution)/shard_map/cas,sb->cab/dot_general | solution.py:32
  58.1 1.3 %convolution_add_fusion.1 = f32[4,32,256]{2,1,0:T(8,128)S(1)} fusion(f32[4,32,256]{2,1,0:T(8,128)S(1)} %fusion.30, f32[32,4,256]{2,0,1:T(8,128)S(1)} %fusion.39, f32[32,4,256]{2,0,1:T(8,128)S(1)} %convolution_negate_fusion, f32[32,256]{1,0:T(8,128)S(1)} %get-tuple-element.7, f32[32,256]{1,0:T(8,128)S(1)} %get-tuple-element.8), kind=kOutput, calls=%fused_computation.8 | convolution fusion | flops 101711872 | bytes 589824 | tf_op jit(solution)/shard_map/cas,sb->cab/dot_general | solution.py:32
  59.4 5.4 %all-to-all-done = f32[32,4,256]{2,1,0:T(4,128)S(1)} async-done(((f32[32,4,256]{2,1,0:T(4,128)}), f32[32,4,256]{2,1,0:T(4,128)S(1)}, u32[]{:S(2)}, u32[]{:S(2)}) %all-to-all-start) | async-done | bytes 131104 | tf_op jit(solution)/shard_map/all_to_all | solution.py:72
  64.8 0.3 convolution_bitcast_fusion
  65.2 0.3 fusion.3
  65.6 1.3 %fusion.32 = f32[4,32,256]{2,1,0:T(8,128)S(1)} fusion(f32[4,32,256]{2,1,0:T(8,128)S(1)} %fusion.3, f32[4,32,256]{2,1,0:T(8,128)S(1)} %convolution_bitcast_fusion, f32[32,256]{1,0:T(8,128)S(1)} %get-tuple-element.7, f32[32,256]{1,0:T(8,128)S(1)} %get-tuple-element.8), kind=kOutput, calls=%fused_computation.46 | convolution fusion | flops 101679104 | bytes 458752 | tf_op jit(solution)/shard_map/cas,sb->cab/dot_general | solution.py:32
  66.8 1.3 %fusion.28 = f32[4,32,256]{2,1,0:T(8,128)S(1)} fusion(f32[4,32,256]{2,1,0:T(8,128)S(1)} %convolution_bitcast_fusion, f32[4,32,256]{2,1,0:T(8,128)S(1)} %fusion.3, f32[32,256]{1,0:T(8,128)S(1)} %get-tuple-element.7, f32[32,256]{1,0:T(8,128)S(1)} %get-tuple-element.8), kind=kOutput, calls=%fused_computation.42 | convolution fusion | flops 101679104 | bytes 458752 | tf_op jit(solution)/shard_map/cas,sb->cab/dot_general | solution.py:35
  68.1 1.3 %convolution_add_fusion.2 = f32[4,32,256]{2,1,0:T(8,128)S(1)} fusion(f32[4,32,256]{2,1,0:T(8,128)S(1)} %fusion.32, f32[4,32,256]{2,1,0:T(8,128)S(1)} %convolution_bitcast_fusion, f32[4,32,256]{2,1,0:T(8,128)S(1)} %fusion.3, f32[32,256]{1,0:T(8,128)S(1)} %get-tuple-element.7, f32[32,256]{1,0:T(8,128)S(1)} %get-tuple-element.8), kind=kOutput, calls=%fused_computation.9 | convolution fusion | flops 101711872 | bytes 589824 | tf_op jit(solution)/shard_map/cas,sb->cab/dot_general | solution.py:32
  69.4 1.3 %multiply_add_fusion = (f32[4,32,256]{2,1,0:T(8,128)S(1)}, f32[4,32,256]{2,1,0:T(8,128)S(1)}) fusion(f32[4,32,256]{2,1,0:T(8,128)S(1)} %convolution_add_fusion.1, f32[4,32,256]{2,1,0:T(8,128)S(1)} %convolution_add_fusion.2, f32[4,32,256]{2,1,0:T(8,128)S(1)} %convolution_subtract_fusion.1, f32[4,32,256]{2,1,0:T(8,128)S(1)} %fusion.28, ...), kind=kOutput, calls=%fused_computation.73 | convolution fusion | flops 101908480 | bytes 1114112 | tf_op jit(solution)/shard_map/cas,sb->cab/dot_general | solution.py:35
  70.7 1.2 %fusion.24 = f32[4,32,256]{2,1,0:T(8,128)S(1)} fusion(f32[4,32,256]{2,1,0:T(8,128)S(1)} %get-tuple-element.6), kind=kOutput, calls=%fused_computation.38 | convolution fusion | flops 101580800 | bytes 262144 | tf_op jit(solution)/shard_map/cab,bs->cas/dot_general | solution.py:43
  71.9 1.3 %fusion.16 = f32[4,32,256]{2,1,0:T(8,128)S(1)} fusion(f32[4,32,256]{2,1,0:T(8,128)S(1)} %get-tuple-element.6), kind=kOutput, calls=%fused_computation.30 | convolution fusion | flops 101580800 | bytes 262144 | tf_op jit(solution)/shard_map/cab,bs->cas/dot_general | solution.py:46
  73.2 1.3 %convolution_subtract_fusion = f32[4,32,256]{2,1,0:T(8,128)S(1)} fusion(f32[4,32,256]{2,1,0:T(8,128)S(1)} %fusion.24, f32[4,32,256]{2,1,0:T(8,128)S(1)} %get-tuple-element.5), kind=kOutput, calls=%fused_computation.5 | convolution fusion | flops 101613568 | bytes 393216 | tf_op jit(solution)/shard_map/cab,bs->cas/dot_general | solution.py:43
  74.4 1.2 %convolution_add_fusion = f32[4,32,256]{2,1,0:T(8,128)S(1)} fusion(f32[4,32,256]{2,1,0:T(8,128)S(1)} %fusion.16, f32[4,32,256]{2,1,0:T(8,128)S(1)} %get-tuple-element.5), kind=kOutput, calls=%fused_computation.4 | convolution fusion | flops 101613568 | bytes 393216 | tf_op jit(solution)/shard_map/cab,bs->cas/dot_general | solution.py:46
  75.7 0.4 fusion.53
  76.1 0.4 fusion.6
  76.5 0.1 copy.15
  76.6 9.9 %all_to_all.32 = f32[4,32,256]{2,0,1:T(4,128)S(1)} all-to-all(f32[4,32,256]{2,0,1:T(4,128)S(1)} %copy.15), channel_id=1, replica_groups=mesh['tm'=4,'nrn'=8] {'tm','nrn'}, dimensions={1} | all-to-all | bytes 262144 | tf_op jit(solution)/shard_map/all_to_all | solution.py:83
  86.5 0.1 copy.16
  86.6 0.1 fusion.41
  86.7 0.0 copy-done.3
  86.7 0.0 copy-done.2
  86.7 0.3 fusion.77
  87.0 0.0 copy-done.5
  87.0 0.0 copy-done.4
  87.0 1.1 %fusion.7 = bf16[256,128]{1,0:T(8,128)(2,1)} fusion(bf16[512,128]{1,0:T(8,128)(2,1)S(1)} %copy-done.4, bf16[128,512]{1,0:T(8,128)(2,1)S(1)} %copy-done.5, f32[256,512]{1,0:T(8,128)S(1)} %fusion.77, f32[128,256]{0,1:T(8,128)S(1)} %copy.16, f32[128]{0:T(128)S(1)} %copy-done.3, f32[256]{0:T(256)S(1)} %add_rsqrt_fusion), kind=kOutput, calls=%fused_computation.18 | convolution fusion | flops 68059136 | bytes 984576 | tf_op jit(solution)/shard_map/dot_general | solution.py:90
  (2 shorter events, 0.1 us)
Async XLA Ops:
  6.5 1.2 %copy-start = (bf16[4096,128]{1,0:T(8,128)(2,1)S(1)}, bf16[4096,128]{1,0:T(8,128)(2,1)}, u32[]{:S(2)}) copy-start(bf16[4096,128]{1,0:T(8,128)(2,1)} %param.8) | copy-start | bytes 3145732
  6.5 10.5 %copy-start.1 = (f32[4,8192]{1,0:T(4,128)S(1)}, f32[4,8192]{1,0:T(4,128)}, u32[]{:S(2)}) copy-start(f32[4,8192]{1,0:T(4,128)} %param.9) | copy-start | bytes 393220
  6.5 80.2 %copy-start.3 = (f32[128]{0:T(128)S(1)}, f32[128]{0:T(128)}, u32[]{:S(2)}) copy-start(f32[128]{0:T(128)} %param.10) | copy-start | bytes 1540
  6.5 80.2 %copy-start.2 = (bf16[128,512]{1,0:T(8,128)(2,1)S(1)}, bf16[128,512]{1,0:T(8,128)(2,1)}, u32[]{:S(2)}) copy-start(bf16[128,512]{1,0:T(8,128)(2,1)} %param.11) | copy-start | bytes 393220
  6.5 80.5 %copy-start.5 = (bf16[128,512]{1,0:T(8,128)(2,1)S(1)}, bf16[128,512]{1,0:T(8,128)(2,1)}, u32[]{:S(2)}) copy-start(bf16[128,512]{1,0:T(8,128)(2,1)} %param.12) | copy-start | bytes 393220
  6.5 80.5 %copy-start.4 = (bf16[512,128]{1,0:T(8,128)(2,1)S(1)}, bf16[512,128]{1,0:T(8,128)(2,1)}, u32[]{:S(2)}) copy-start(bf16[512,128]{1,0:T(8,128)(2,1)} %param.13) | copy-start | bytes 393220
  6.6 45.6 %reduce-scatter.2.cloned.1.call-start = ((), (), s32[]{:S(2)}) async-start(), calls=%async_computation.3 | async-start | bytes 1179648 | tf_op jit(solution)/shard_map/reduce_scatter | solution.py:65
  53.8 11.0 %all-to-all-start = ((f32[32,4,256]{2,1,0:T(4,128)}), f32[32,4,256]{2,1,0:T(4,128)S(1)}, u32[]{:S(2)}, u32[]{:S(2)}) async-start(f32[32,4,256]{2,1,0:T(4,128)} %all_to_all.24), calls=%async_computation.1 | async-start | bytes 262144 | tf_op jit(solution)/shard_map/all_to_all | solution.py:72
Sparse Core Ops, SparseCore 0:
  17.0 35.0 reduce-scatter.1
where the time goes:
time: 95.1 us; the launch traced here: 94.9 us
  waiting for transfers between devices  37.3 us (39%)
  matrix products  27.7 us (29%)
  between operations  13.6 us (14%)
  blocking collectives  9.88 us (10%)
  local copies, waits for them, and re-layouts  3.09 us (3%)
  starting transfers between devices  3.08 us (3%)
    reduce_scatter x1, waiting for transfers between devices, per_device(): lax.psum_scatter(jnp.dot(spikes, read_in, preferred_element_type=jnp.floa...  31.8 us
    all_to_all x1, blocking collectives, per_device(): lax.all_to_all(mixed, ('tm', 'nrn'), split_axis=1, concat_axis=0, tiled=T...  9.88 us
    dot_general x1, matrix products, per_device(): jnp.dot(spikes, read_in, preferred_element_type=jnp.float32)  9.09 us
    all_to_all x1, waiting for transfers between devices, per_device(): lax.all_to_all(flipped, ('tm', 'nrn'), split_axis=0, concat_axis=1, tiled...  5.45 us
    all_to_all x1, starting transfers between devices, per_device(): lax.all_to_all(flipped, ('tm', 'nrn'), split_axis=0, concat_axis=1, tiled...  3.04 us
    dot_general x2, matrix products, forward_dft(): jnp.einsum('cas,sb->cab', twist_real, sin_inner, precision=precise)  2.55 us
    dot_general x2, matrix products, forward_dft(): jnp.einsum('cas,sb->cab', twist_imag, sin_inner, precision=precise)  2.54 us
    dot_general x2, matrix products, forward_dft(): jnp.einsum('cas,sb->cab', twist_real, cos_inner, precision=precise)  2.53 us
  transfers between devices with their start and end apart: 2, of which 2 were waited for; matrix products, arithmetic and copies ran while one was open for 6% of the time, Pallas kernels for 0%

commit v1 on v0

--- a/solution.py
+++ b/solution.py
@@ -2,8 +2,18 @@
 
 import jax
 import jax.numpy as jnp
+import ml_dtypes
+import numpy as np
 from jax import lax
+from jax.experimental import pallas as pl
+from jax.experimental.pallas import tpu as pltpu
 from jax.sharding import PartitionSpec as P
+
+MESH = pl.DeviceIdType.MESH
+TILE_BINS = 1
+TILES = 8
+AHEAD = 3
+LAG = 5
 
 precise = lax.Precision.HIGHEST
 
@@ -92,8 +102,361 @@
     )
 
 
+def split(value):
+    high = value.astype(jnp.bfloat16)
+    low = (value - high.astype(jnp.float32)).astype(jnp.bfloat16)
+    return high, low
+
+
+def session_tables():
+    outer, inner = 32, 256
+    angle = lambda rows, columns, order: (
+        2.0 * np.pi / order * (np.outer(np.arange(rows), np.arange(columns)) % order)
+    )
+
+    def parts(table):
+        table = table.astype(np.float32)
+        high = table.astype(ml_dtypes.bfloat16)
+        low = (table - high.astype(np.float32)).astype(ml_dtypes.bfloat16)
+        return high, low
+
+    around = angle(outer, outer, outer)
+    high, low = parts(np.concatenate([np.cos(around), -np.sin(around)], 0))
+    first = np.concatenate([high, low, high], 1)
+    high, low = parts(np.concatenate([np.cos(around), -np.sin(around)], 1))
+    last = np.concatenate([high, low, high], 1)
+    within = angle(inner, inner, inner)
+    cosine, sine = np.cos(within), np.sin(within)
+    mid_high, mid_low = parts(np.block([[cosine, -sine], [sine, cosine]]))
+    turn = angle(outer, inner, outer * inner)
+    twist = np.stack([np.cos(turn), np.sin(turn)]).astype(np.float32)
+    return first, last, np.stack([mid_high, mid_low]), twist
+
+
+def fused_kernel(
+    spikes, read_in, kernel, gain, w_gate, w_up, w_down, first, last, middle, twist,
+    out,
+    spk_v, rd_v, ker_v, wg_v, wu_v, wd_v, first_v, last_v, mid_v, twist_v,
+    own, sib, acc, from_end, fwd, from_inner, to_end, from_mid, xsend, xall, kall, ysend, yall, spec,
+    spk_sem, tab_sem, sib_s, sib_r, end_s, end_r, inn_s, inn_r, fin_s, fin_r, x_s, x_r, y_s, y_r,
+):
+    tm, nrn = lax.axis_index("tm"), lax.axis_index("nrn")
+    me = tm * 8 + nrn
+    z, core = nrn // 2, nrn % 2
+    is_end = (z == 0) | (z == 3)
+    is_inner = (z == 1) | (z == 2)
+    rows = TILE_BINS * 256
+
+    def spike_copy(k):
+        return pltpu.make_async_copy(
+            spikes.at[pl.ds(pl.multiple_of(k * rows, rows), rows)], spk_v.at[k], spk_sem.at[k]
+        )
+
+    loads = [
+        pltpu.make_async_copy(source, target, tab_sem.at[i])
+        for i, (source, target) in enumerate(
+            [
+                (read_in, rd_v), (kernel, ker_v), (first, first_v), (twist, twist_v),
+                (middle, mid_v), (last, last_v), (w_gate, wg_v), (w_up, wu_v), (w_down, wd_v),
+            ]
+        )
+    ]
+    loads[0].start()
+    for k in range(AHEAD):
+        spike_copy(k).start()
+    for load in loads[1:]:
+        load.start()
+
+    barrier = pltpu.get_barrier_semaphore()
+
+    def greet(d, carry):
+        other = (me + d) % 32
+        pl.semaphore_signal(barrier, inc=1, device_id=(other // 8, other % 8), device_id_type=MESH)
+        return carry
+
+    lax.fori_loop(1, 32, greet, 0)
+    loads[0].wait()
+    pl.semaphore_wait(barrier, 31)
+
+    def remote(source, target, send, recv, where):
+        return pltpu.make_async_remote_copy(
+            src_ref=source, dst_ref=target, send_sem=send, recv_sem=recv,
+            device_id=where, device_id_type=MESH,
+        )
+
+    def at_z(place):
+        return (tm, place * 2 + core)
+
+    def sib_copy(k):
+        return remote(own.at[k, 1 - core], sib.at[k], sib_s.at[k], sib_r.at[k], (tm, z * 2 + 1 - core))
+
+    end_inner = jnp.where(z == 0, 1, 2)
+    end_first = jnp.where(z == 0, 1, 0)
+    near_end = jnp.where(z == 1, 0, 3)
+    fwd_first = jnp.where(z == 1, 2, 0)
+    own_slot = z % 2
+
+    def end_copy(k):
+        return remote(
+            acc.at[k, pl.ds(end_first, 3)], from_end.at[k, pl.ds(end_first, 3)],
+            end_s.at[k], end_r.at[k], at_z(end_inner),
+        )
+
+    def inner_copy(k):
+        return remote(fwd.at[k], from_inner.at[k], inn_s.at[k], inn_r.at[k], at_z(3 - z))
+
+    def final_copy(k):
+        return remote(to_end.at[k], from_mid.at[k], fin_s.at[k], fin_r.at[k], at_z(near_end))
+
+    def x_copy(k, d):
+        other = (tm + d) % 4
+        return remote(
+            xsend.at[k, other], xall.at[pl.ds(tm * 8 + k * TILE_BINS, TILE_BINS)],
+            x_s.at[k, d], x_r.at[k, d], (other, nrn),
+        )
+
+    def project(k):
+        spike_copy(k).wait()
+        sums = jnp.dot(spk_v[k], rd_v[...], preferred_element_type=jnp.float32)
+        for b in range(TILE_BINS):
+            low = sums[b * 256 : b * 256 + 128].T
+            high = sums[b * 256 + 128 : b * 256 + 256].T
+            for g in range(32):
+                piece = jnp.concatenate([low[4 * g : 4 * g + 4], high[4 * g : 4 * g + 4]], 0)
+                own[k, g % 2, (g % 8) // 2, g // 8, b] = piece
+        sib_copy(k).start()
+
+    def pair(k):
+        sib_copy(k).wait_recv()
+        acc[k] = own[k, core] + sib[k]
+
+        @pl.when(is_end)
+        def _():
+            end_copy(k).start()
+
+    def forward_sum(k):
+        @pl.when(is_inner)
+        def _():
+            end_copy(k).wait_recv()
+            fwd[k] = acc[k, pl.ds(fwd_first, 2)] + from_end[k, pl.ds(fwd_first, 2)]
+            inner_copy(k).start()
+
+    def finish_sum(k):
+        @pl.when(is_inner)
+        def _():
+            inner_copy(k).wait_recv()
+            to_end[k] = acc[k, near_end] + from_inner[k, 1 - own_slot]
+            final_copy(k).start()
+            xsend[k] = acc[k, z] + from_end[k, z] + from_inner[k, own_slot]
+
+        @pl.when(is_end)
+        def _():
+            final_copy(k).wait_recv()
+            xsend[k] = acc[k, z] + from_mid[k]
+
+        for d in (3, 1, 2):
+            x_copy(k, d).start()
+        xall[pl.ds(tm * 8 + k * TILE_BINS, TILE_BINS)] = xsend[k, tm]
+
+    def tile_step(k, carry):
+        @pl.when(k + AHEAD < TILES)
+        def _():
+            spike_copy(k + AHEAD).start()
+
+        project(k)
+
+        @pl.when(k >= 1)
+        def _():
+            pair(k - 1)
+
+        @pl.when(k >= LAG)
+        def _():
+            forward_sum(k - LAG)
+
+        return carry
+
+    lax.fori_loop(0, TILES, tile_step, 0)
+    pair(TILES - 1)
+
+    for load in loads[1:]:
+        load.wait()
+    for r in range(32):
+        for half in range(2):
+            kall[r, half * 4 : half * 4 + 4, :] = ker_v[:, r * 256 + half * 128 : r * 256 + half * 128 + 128]
+
+    cos_turn = jnp.concatenate([twist_v[0]] * 4, 1)
+    sin_turn = jnp.concatenate([twist_v[1]] * 4, 1)
+
+    def stacked(value):
+        high, low = split(value)
+        return jnp.concatenate([high, high, low], 0)
+
+    def to_rows(value):
+        return jnp.concatenate([value[:, 256 * j : 256 * j + 256] for j in range(4)], 0)
+
+    def to_lanes(value):
+        return jnp.concatenate([value[32 * j : 32 * j + 32] for j in range(4)], 1)
+
+    def inner_dft(real, imag):
+        high, low = split(jnp.concatenate([real, imag], 1))
+        result = jnp.dot(high, mid_v[0], preferred_element_type=jnp.float32)
+        result += jnp.dot(high, mid_v[1], preferred_element_type=jnp.float32)
+        result += jnp.dot(low, mid_v[0], preferred_element_type=jnp.float32)
+        return result[:, :256], result[:, 256:]
+
+    def gather_lanes(ref):
+        return jnp.concatenate([ref[:, half * 4 + j, :] for j in range(4) for half in range(2)], 1)
+
+    def forward_dft(signal):
+        both = jnp.dot(first_v[...], stacked(signal), preferred_element_type=jnp.float32)
+        real, imag = both[:32], both[32:]
+        turned_real = real * cos_turn + imag * sin_turn
+        turned_imag = imag * cos_turn - real * sin_turn
+        return inner_dft(to_rows(turned_real), to_rows(turned_imag))
+
+    kern_real, kern_imag = forward_dft(gather_lanes(kall))
+    spec[0] = kern_real * (1.0 / 8192)
+    spec[1] = kern_imag * (1.0 / 8192)
+
+    def late_forward(k, carry):
+        forward_sum(k)
+
+        @pl.when(k > TILES - LAG)
+        def _():
+            finish_sum(k - 1)
+
+        return carry
+
+    def early_finish(k, carry):
+        finish_sum(k)
+        return carry
+
+    lax.fori_loop(TILES - LAG, TILES - LAG + 1, late_forward, 0)
+    lax.fori_loop(0, TILES - LAG, early_finish, 0)
+    lax.fori_loop(TILES - LAG + 1, TILES, late_forward, 0)
+    finish_sum(TILES - 1)
+
+    def x_arrived(k, carry):
+        for d in (1, 2, 3):
+            x_copy(k, d).wait_recv()
+        return carry
+
+    lax.fori_loop(0, TILES, x_arrived, 0)
+
+    series = gather_lanes(xall)
+    data_real, data_imag = forward_dft(series)
+    prod_real = data_real * spec[0] - data_imag * spec[1]
+    prod_imag = data_real * spec[1] + data_imag * spec[0]
+    back_real, back_neg = inner_dft(prod_real, -prod_imag)
+    back_real, back_neg = to_lanes(back_real), to_lanes(back_neg)
+    turned = jnp.concatenate(
+        [back_real * cos_turn + back_neg * sin_turn, back_real * sin_turn - back_neg * cos_turn], 0
+    )
+    mixed = series + jnp.dot(last_v[...], stacked(turned), preferred_element_type=jnp.float32)
+    for m in range(8):
+        ysend[:, m, :] = mixed[:, 128 * m : 128 * m + 128]
+
+    def y_copy(d):
+        other = (me + d) % 32
+        return remote(ysend.at[other], yall.at[me], y_s.at[d], y_r.at[d], (other // 8, other % 8))
+
+    def y_start(d, carry):
+        y_copy(d).start()
+        return carry
+
+    lax.fori_loop(1, 32, y_start, 0)
+    yall[me] = ysend[me]
+
+    def drain(k, carry):
+        sib_copy(k).wait_send()
+
+        @pl.when(is_end)
+        def _():
+            end_copy(k).wait_send()
+
+        @pl.when(is_inner)
+        def _():
+            inner_copy(k).wait_send()
+            final_copy(k).wait_send()
+
+        for d in (1, 2, 3):
+            x_copy(k, d).wait_send()
+        return carry
+
+    lax.fori_loop(0, TILES, drain, 0)
+
+    def y_wait(d, carry):
+        y_copy(d).wait()
+        return carry
+
+    lax.fori_loop(1, 32, y_wait, 0)
+
+    flat = yall.reshape(256, 128)
+    residual = jnp.concatenate([flat[pl.ds(half, 128, stride=2), :].T for half in range(2)], 0)
+    meansq = jnp.mean(residual * residual, axis=-1, keepdims=True)
+    normed = (residual * lax.rsqrt(meansq + 1e-05) * gain[...]).astype(jnp.bfloat16)
+    gate = jnp.dot(normed, wg_v[...], preferred_element_type=jnp.float32)
+    upper = jnp.dot(normed, wu_v[...], preferred_element_type=jnp.float32)
+    act = (gate / (1.0 + jnp.exp(-gate)) * upper).astype(jnp.bfloat16)
+    out[...] = (residual + jnp.dot(act, wd_v[...], preferred_element_type=jnp.float32)).astype(jnp.bfloat16)
+
+
+def fused(spikes, read_in, kernel, gain, w_gate, w_up, w_down):
+    first, last, middle, twist = session_tables()
+    f32, bf16 = jnp.float32, jnp.bfloat16
+    tile = (TILE_BINS, 8, 128)
+    rows = TILE_BINS * 256
+    dma = pltpu.SemaphoreType.DMA
+    anywhere = pl.BlockSpec(memory_space=pl.ANY)
+    vmem = pl.BlockSpec(memory_space=pltpu.VMEM)
+    return pl.pallas_call(
+        fused_kernel,
+        out_shape=jax.ShapeDtypeStruct((256, 128), bf16),
+        in_specs=[anywhere] * 3 + [vmem] + [anywhere] * 7,
+        out_specs=vmem,
+        scratch_shapes=[
+            pltpu.VMEM((TILES, rows, 4096), bf16),
+            pltpu.VMEM((4096, 128), bf16),
+            pltpu.VMEM((4, 8192), f32),
+            pltpu.VMEM((128, 512), bf16),
+            pltpu.VMEM((128, 512), bf16),
+            pltpu.VMEM((512, 128), bf16),
+            pltpu.VMEM(first.shape, bf16),
+            pltpu.VMEM(last.shape, bf16),
+            pltpu.VMEM(middle.shape, bf16),
+            pltpu.VMEM(twist.shape, f32),
+            pltpu.VMEM((TILES, 2, 4, 4) + tile, f32),
+            pltpu.VMEM((TILES, 4, 4) + tile, f32),
+            pltpu.VMEM((TILES, 4, 4) + tile, f32),
+            pltpu.VMEM((TILES, 4, 4) + tile, f32),
+            pltpu.VMEM((TILES, 2, 4) + tile, f32),
+            pltpu.VMEM((TILES, 2, 4) + tile, f32),
+            pltpu.VMEM((TILES, 4) + tile, f32),
+            pltpu.VMEM((TILES, 4) + tile, f32),
+            pltpu.VMEM((TILES, 4) + tile, f32),
+            pltpu.VMEM((32, 8, 128), f32),
+            pltpu.VMEM((32, 8, 128), f32),
+            pltpu.VMEM((32, 8, 128), f32),
+            pltpu.VMEM((32, 8, 128), f32),
+            pltpu.VMEM((2, 128, 256), f32),
+            dma((TILES,)), dma((9,)),
+            dma((TILES,)), dma((TILES,)), dma((TILES,)), dma((TILES,)),
+            dma((TILES,)), dma((TILES,)), dma((TILES,)), dma((TILES,)),
+            dma((TILES, 4)), dma((TILES, 4)), dma((32,)), dma((32,)),
+        ],
+        compiler_params=pltpu.CompilerParams(
+            collective_id=0, has_side_effects=True, vmem_limit_bytes=56 * 1024 * 1024
+        ),
+    )(
+        spikes, read_in, kernel, gain.reshape(1, 128), w_gate, w_up, w_down,
+        jnp.asarray(first), jnp.asarray(last), jnp.asarray(middle), jnp.asarray(twist),
+    )
+
+
 def solution(mesh):
     placed = (P("tm", "nrn"), P("nrn", None), P(("tm", "nrn"), None), P(), P(), P(), P())
+    small = mesh.shape["tm"] == 4 and mesh.shape["nrn"] == 8
     return jax.shard_map(
-        per_device, mesh=mesh, in_specs=placed, out_specs=P(("tm", "nrn"), None), check_vma=False
-    )
+        fused if small else per_device,
+        mesh=mesh, in_specs=placed, out_specs=P(("tm", "nrn"), None), check_vma=False,
+    )

time: 95.1 us -> 41.4 us (0.44)
  Pallas kernels: 0 us -> 39.7 us
  waiting for transfers between devices: 37.3 us -> 0 us
  matrix products: 27.7 us -> 0 us
  between operations: 13.6 us -> 0.01 us
  blocking collectives: 9.88 us -> 0 us
  starting transfers between devices: 3.08 us -> 0 us
  local copies, waits for them, and re-layouts: 3.09 us -> 1.47 us
    pallas_call x0 -> x1, Pallas kernels: none -> 39.7 us  [fused(): pl.pallas_call(fused_kernel, out_shape=jax.ShapeDtypeStruct((256, 128), b...]
    reduce_scatter x1 -> x0, waiting for transfers between devices: 31.8 us -> none  [per_device(): lax.psum_scatter(jnp.dot(spikes, read_in, preferred_element_type=jnp.floa...]
    dot_general x21 -> x0, matrix products: 27.7 us -> none  [the longest x1 9.09 us: per_device(): jnp.dot(spikes, read_in, preferred_element_type=jnp.float32)]
    all_to_all x1 -> x0, blocking collectives: 9.88 us -> none  [per_device(): lax.all_to_all(mixed, ('tm', 'nrn'), split_axis=1, concat_axis=0, tiled=T...]
    all_to_all x1 -> x0, waiting for transfers between devices: 5.45 us -> none  [per_device(): lax.all_to_all(flipped, ('tm', 'nrn'), split_axis=0, concat_axis=1, tiled...]
    all_to_all x1 -> x0, starting transfers between devices: 3.04 us -> none  [per_device(): lax.all_to_all(flipped, ('tm', 'nrn'), split_axis=0, concat_axis=1, tiled...]
    transpose x1 -> x0, local copies, waits for them, and re-layouts: 1 us -> none  [per_device(): flipped = latent.T]
  transfers between devices with their start and end apart: 2 -> 0, of which waited for: 2 -> 0; matrix products, arithmetic and copies ran while one was open for 6% -> 0% of each run, Pallas kernels for 0% -> 0%
where the time goes in v1:
time: 41.4 us; the launch traced here: 41.2 us
  Pallas kernels  39.7 us (96%)
  local copies, waits for them, and re-layouts  1.47 us (4%)
    pallas_call x1, Pallas kernels, fused(): pl.pallas_call(fused_kernel, out_shape=jax.ShapeDtypeStruct((256, 128), b...  39.7 us
    unnamed x1, local copies, waits for them, and re-layouts  1.47 us

profile of v1, /device:TPU:0, one launch (start us, length us, event | category | flops | bytes accessed | tf_op | source)
XLA Modules:
  0.0 41.2 jit_solution(9161018998707467753)
XLA Ops:
  0.0 39.7 %shard_map.109 = bf16[256,128]{1,0:T(8,128)(2,1)} custom-call(bf16[2048,4096]{1,0:T(8,128)(2,1)} %spikes.1, bf16[4096,128]{1,0:T(8,128)(2,1)} %read_in.1, f32[4,8192]{1,0:T(4,128)} %kernel.1, f32[1,128]{1,0:T(1,128)} %bitcast.1, bf16[128,512]{1,0:T(8,128)(2,1)} %w_gate.1, bf16[128,512]{1,0:T(8,128)(2,1)} %w_up.1, bf16[512,128]{1,0:T(8,128)(2,1)} %w_down.1, ...), custom_call_target="tpu_custom_call" | custom-call | tf_op jit(solution)/shard_map/pallas_call | solution.py:412
  39.8 1.5 %copy.13 = bf16[256,128]{1,0:T(8,128)(2,1)} copy(bf16[256,128]{1,0:T(8,128)(2,1)} %shard_map.109) | data formatting | bytes 131072

commit v2 on v1

--- a/solution.py
+++ b/solution.py
@@ -12,8 +12,6 @@
 MESH = pl.DeviceIdType.MESH
 TILE_BINS = 1
 TILES = 8
-AHEAD = 3
-LAG = 5
 
 precise = lax.Precision.HIGHEST
 
@@ -142,15 +140,14 @@
 ):
     tm, nrn = lax.axis_index("tm"), lax.axis_index("nrn")
     me = tm * 8 + nrn
-    z, core = nrn // 2, nrn % 2
+    z, core = lax.div(nrn, 2), lax.rem(nrn, 2)
     is_end = (z == 0) | (z == 3)
     is_inner = (z == 1) | (z == 2)
     rows = TILE_BINS * 256
 
     def spike_copy(k):
-        return pltpu.make_async_copy(
-            spikes.at[pl.ds(pl.multiple_of(k * rows, rows), rows)], spk_v.at[k], spk_sem.at[k]
-        )
+        where = pl.ds(k * rows, rows)
+        return pltpu.make_async_copy(spikes.at[where], spk_v.at[where], spk_sem.at[k])
 
     loads = [
         pltpu.make_async_copy(source, target, tab_sem.at[i])
@@ -162,16 +159,17 @@
         )
     ]
     loads[0].start()
-    for k in range(AHEAD):
+    for k in range(4):
         spike_copy(k).start()
-    for load in loads[1:]:
-        load.start()
 
     barrier = pltpu.get_barrier_semaphore()
 
+    def after(d):
+        other = lax.rem(me + d, 32)
+        return (lax.div(other, 8), lax.rem(other, 8))
+
     def greet(d, carry):
-        other = (me + d) % 32
-        pl.semaphore_signal(barrier, inc=1, device_id=(other // 8, other % 8), device_id_type=MESH)
+        pl.semaphore_signal(barrier, inc=1, device_id=after(d), device_id_type=MESH)
         return carry
 
     lax.fori_loop(1, 32, greet, 0)
@@ -194,7 +192,7 @@
     end_first = jnp.where(z == 0, 1, 0)
     near_end = jnp.where(z == 1, 0, 3)
     fwd_first = jnp.where(z == 1, 2, 0)
-    own_slot = z % 2
+    own_slot = lax.rem(z, 2)
 
     def end_copy(k):
         return remote(
@@ -209,22 +207,25 @@
         return remote(to_end.at[k], from_mid.at[k], fin_s.at[k], fin_r.at[k], at_z(near_end))
 
     def x_copy(k, d):
-        other = (tm + d) % 4
+        other = lax.rem(tm + d, 4)
         return remote(
             xsend.at[k, other], xall.at[pl.ds(tm * 8 + k * TILE_BINS, TILE_BINS)],
             x_s.at[k, d], x_r.at[k, d], (other, nrn),
         )
 
-    def project(k):
-        spike_copy(k).wait()
-        sums = jnp.dot(spk_v[k], rd_v[...], preferred_element_type=jnp.float32)
-        for b in range(TILE_BINS):
-            low = sums[b * 256 : b * 256 + 128].T
-            high = sums[b * 256 + 128 : b * 256 + 256].T
-            for g in range(32):
-                piece = jnp.concatenate([low[4 * g : 4 * g + 4], high[4 * g : 4 * g + 4]], 0)
-                own[k, g % 2, (g % 8) // 2, g // 8, b] = piece
-        sib_copy(k).start()
+    def project(start, count):
+        for k in range(start, start + count):
+            spike_copy(k).wait()
+        block = spk_v[start * rows : (start + count) * rows]
+        sums = jnp.dot(block, rd_v[...], preferred_element_type=jnp.float32)
+        for i in range(count):
+            for b in range(TILE_BINS):
+                at = i * rows + b * 256
+                low, high = sums[at : at + 128].T, sums[at + 128 : at + 256].T
+                for g in range(32):
+                    piece = jnp.concatenate([low[4 * g : 4 * g + 4], high[4 * g : 4 * g + 4]], 0)
+                    own[start + i, g % 2, (g % 8) // 2, g // 8, b] = piece
+            sib_copy(start + i).start()
 
     def pair(k):
         sib_copy(k).wait_recv()
@@ -258,25 +259,29 @@
             x_copy(k, d).start()
         xall[pl.ds(tm * 8 + k * TILE_BINS, TILE_BINS)] = xsend[k, tm]
 
-    def tile_step(k, carry):
-        @pl.when(k + AHEAD < TILES)
-        def _():
-            spike_copy(k + AHEAD).start()
-
-        project(k)
-
-        @pl.when(k >= 1)
-        def _():
-            pair(k - 1)
-
-        @pl.when(k >= LAG)
-        def _():
-            forward_sum(k - LAG)
-
-        return carry
-
-    lax.fori_loop(0, TILES, tile_step, 0)
-    pair(TILES - 1)
+    def each(step, start, stop):
+        def body(k, carry):
+            step(k)
+            return carry
+
+        lax.fori_loop(start, stop, body, 0)
+
+    project(0, 1)
+    for k in range(4, TILES):
+        spike_copy(k).start()
+    for load in loads[1:]:
+        load.start()
+    project(1, 1)
+    pair(0)
+    project(2, 2)
+    pair(1)
+    project(4, 2)
+    each(pair, 2, 4)
+    each(forward_sum, 0, 2)
+    project(6, 2)
+    each(pair, 4, 6)
+    forward_sum(2)
+    each(pair, 6, 8)
 
     for load in loads[1:]:
         load.wait()
@@ -299,42 +304,36 @@
 
     def inner_dft(real, imag):
         high, low = split(jnp.concatenate([real, imag], 1))
-        result = jnp.dot(high, mid_v[0], preferred_element_type=jnp.float32)
+        both = jnp.concatenate([high, low], 0)
+        result = jnp.dot(both, mid_v[0], preferred_element_type=jnp.float32)
+        result = result[:128] + result[128:]
         result += jnp.dot(high, mid_v[1], preferred_element_type=jnp.float32)
-        result += jnp.dot(low, mid_v[0], preferred_element_type=jnp.float32)
         return result[:, :256], result[:, 256:]
 
     def gather_lanes(ref):
         return jnp.concatenate([ref[:, half * 4 + j, :] for j in range(4) for half in range(2)], 1)
 
-    def forward_dft(signal):
+    def outer_dft(signal):
         both = jnp.dot(first_v[...], stacked(signal), preferred_element_type=jnp.float32)
         real, imag = both[:32], both[32:]
         turned_real = real * cos_turn + imag * sin_turn
         turned_imag = imag * cos_turn - real * sin_turn
-        return inner_dft(to_rows(turned_real), to_rows(turned_imag))
-
-    kern_real, kern_imag = forward_dft(gather_lanes(kall))
+        return to_rows(turned_real), to_rows(turned_imag)
+
+    spec[0], spec[1] = outer_dft(gather_lanes(kall))
+
+    def forward_then_finish(k):
+        forward_sum(k)
+        finish_sum(k - 2)
+
+    forward_sum(3)
+    each(finish_sum, 0, 2)
+    each(forward_then_finish, 4, 6)
+    kern_real, kern_imag = inner_dft(spec[0], spec[1])
     spec[0] = kern_real * (1.0 / 8192)
     spec[1] = kern_imag * (1.0 / 8192)
-
-    def late_forward(k, carry):
-        forward_sum(k)
-
-        @pl.when(k > TILES - LAG)
-        def _():
-            finish_sum(k - 1)
-
-        return carry
-
-    def early_finish(k, carry):
-        finish_sum(k)
-        return carry
-
-    lax.fori_loop(TILES - LAG, TILES - LAG + 1, late_forward, 0)
-    lax.fori_loop(0, TILES - LAG, early_finish, 0)
-    lax.fori_loop(TILES - LAG + 1, TILES, late_forward, 0)
-    finish_sum(TILES - 1)
+    each(forward_then_finish, 6, 8)
+    each(finish_sum, 6, 8)
 
     def x_arrived(k, carry):
         for d in (1, 2, 3):
@@ -344,7 +343,7 @@
     lax.fori_loop(0, TILES, x_arrived, 0)
 
     series = gather_lanes(xall)
-    data_real, data_imag = forward_dft(series)
+    data_real, data_imag = inner_dft(*outer_dft(series))
     prod_real = data_real * spec[0] - data_imag * spec[1]
     prod_imag = data_real * spec[1] + data_imag * spec[0]
     back_real, back_neg = inner_dft(prod_real, -prod_imag)
@@ -357,14 +356,11 @@
         ysend[:, m, :] = mixed[:, 128 * m : 128 * m + 128]
 
     def y_copy(d):
-        other = (me + d) % 32
-        return remote(ysend.at[other], yall.at[me], y_s.at[d], y_r.at[d], (other // 8, other % 8))
-
-    def y_start(d, carry):
+        other = lax.rem(me + d, 32)
+        return remote(ysend.at[other], yall.at[me], y_s.at[d], y_r.at[d], after(d))
+
+    for d in range(1, 32):
         y_copy(d).start()
-        return carry
-
-    lax.fori_loop(1, 32, y_start, 0)
     yall[me] = ysend[me]
 
     def drain(k, carry):
@@ -398,7 +394,7 @@
     gate = jnp.dot(normed, wg_v[...], preferred_element_type=jnp.float32)
     upper = jnp.dot(normed, wu_v[...], preferred_element_type=jnp.float32)
     act = (gate / (1.0 + jnp.exp(-gate)) * upper).astype(jnp.bfloat16)
-    out[...] = (residual + jnp.dot(act, wd_v[...], preferred_element_type=jnp.float32)).astype(jnp.bfloat16)
+    out[...] = residual + jnp.dot(act, wd_v[...], preferred_element_type=jnp.float32)
 
 
 def fused(spikes, read_in, kernel, gain, w_gate, w_up, w_down):
@@ -411,11 +407,11 @@
     vmem = pl.BlockSpec(memory_space=pltpu.VMEM)
     return pl.pallas_call(
         fused_kernel,
-        out_shape=jax.ShapeDtypeStruct((256, 128), bf16),
+        out_shape=jax.ShapeDtypeStruct((256, 128), f32),
         in_specs=[anywhere] * 3 + [vmem] + [anywhere] * 7,
         out_specs=vmem,
         scratch_shapes=[
-            pltpu.VMEM((TILES, rows, 4096), bf16),
+            pltpu.VMEM((TILES * rows, 4096), bf16),
             pltpu.VMEM((4096, 128), bf16),
             pltpu.VMEM((4, 8192), f32),
             pltpu.VMEM((128, 512), bf16),
@@ -450,7 +446,7 @@
     )(
         spikes, read_in, kernel, gain.reshape(1, 128), w_gate, w_up, w_down,
         jnp.asarray(first), jnp.asarray(last), jnp.asarray(middle), jnp.asarray(twist),
-    )
+    ).astype(bf16)
 
 
 def solution(mesh):

time: 41.4 us -> 42.7 us (1.031)
  other arithmetic: 0 us -> 1.54 us
  local copies, waits for them, and re-layouts: 1.47 us -> 0 us
  Pallas kernels: 39.7 us -> 41 us
    convert_element_type x0 -> x1, other arithmetic: none -> 1.54 us  [fused(): return pl.pallas_call(fused_kernel, out_shape=jax.ShapeDtypeStruct((256,...]
    unnamed x1 -> x0, local copies, waits for them, and re-layouts: 1.47 us -> none
    pallas_call x1, Pallas kernels: 39.7 us -> 41 us  [fused(): pl.pallas_call(fused_kernel, out_shape=jax.ShapeDtypeStruct((256, 128), f...]
where the time goes in v2:
time: 42.7 us; the launch traced here: 42.6 us
  Pallas kernels  41 us (96%)
  other arithmetic  1.54 us (4%)
    pallas_call x1, Pallas kernels, fused(): pl.pallas_call(fused_kernel, out_shape=jax.ShapeDtypeStruct((256, 128), f...  41 us
    convert_element_type x1, other arithmetic, fused(): return pl.pallas_call(fused_kernel, out_shape=jax.ShapeDtypeStruct((256,...  1.54 us

profile of v2, /device:TPU:0, one launch (start us, length us, event | category | flops | bytes accessed | tf_op | source)
XLA Modules:
  0.0 42.6 jit_solution(15662275958870574204)
XLA Ops:
  0.0 41.0 %shard_map.109 = f32[256,128]{1,0:T(8,128)} custom-call(bf16[2048,4096]{1,0:T(8,128)(2,1)} %spikes.1, bf16[4096,128]{1,0:T(8,128)(2,1)} %read_in.1, f32[4,8192]{1,0:T(4,128)} %kernel.1, f32[1,128]{1,0:T(1,128)} %bitcast.1, bf16[128,512]{1,0:T(8,128)(2,1)} %w_gate.1, bf16[128,512]{1,0:T(8,128)(2,1)} %w_up.1, bf16[512,128]{1,0:T(8,128)(2,1)} %w_down.1, ...), custom_call_target="tpu_custom_call" | custom-call | tf_op jit(solution)/shard_map/pallas_call | solution.py:408
  41.0 1.5 %convert_element_type.3 = bf16[256,128]{1,0:T(8,128)(2,1)} convert(f32[256,128]{1,0:T(8,128)} %shard_map.109) | non-fusion elementwise | flops 32768 | bytes 196608 | tf_op jit(solution)/shard_map/convert_element_type | solution.py:449

commit v3 on v2

--- a/solution.py
+++ b/solution.py
@@ -12,6 +12,8 @@
 MESH = pl.DeviceIdType.MESH
 TILE_BINS = 1
 TILES = 8
+AHEAD = 4
+LAG = 4
 
 precise = lax.Precision.HIGHEST
 
@@ -90,6 +92,10 @@
     mixed = series + conv
     stacked = lax.all_to_all(mixed, ("tm", "nrn"), split_axis=1, concat_axis=0, tiled=True)
     residual = stacked.T
+    return gated_mlp(residual, gain, w_gate, w_up, w_down)
+
+
+def gated_mlp(residual, gain, w_gate, w_up, w_down):
     meansq = jnp.mean(residual * residual, axis=-1, keepdims=True)
     normed = (residual * lax.rsqrt(meansq + 1e-05) * gain).astype(jnp.bfloat16)
     gate = jnp.dot(normed, w_gate, preferred_element_type=jnp.float32)
@@ -132,34 +138,32 @@
 
 
 def fused_kernel(
-    spikes, read_in, kernel, gain, w_gate, w_up, w_down, first, last, middle, twist,
+    spikes, read_in, kernel, first, last, middle, twist,
     out,
-    spk_v, rd_v, ker_v, wg_v, wu_v, wd_v, first_v, last_v, mid_v, twist_v,
-    own, sib, acc, from_end, fwd, from_inner, to_end, from_mid, xsend, xall, kall, ysend, yall, spec,
-    spk_sem, tab_sem, sib_s, sib_r, end_s, end_r, inn_s, inn_r, fin_s, fin_r, x_s, x_r, y_s, y_r,
+    spk_v, rd_v, ker_v, first_v, last_v, mid_v, twist_v,
+    own, sib, acc, parts, xsend, xall, ysend, yall, spec, work,
+    spk_sem, tab_sem, sib_s, sib_r, z_s, z_r, x_s, x_r, y_s, y_r,
 ):
     tm, nrn = lax.axis_index("tm"), lax.axis_index("nrn")
     me = tm * 8 + nrn
     z, core = lax.div(nrn, 2), lax.rem(nrn, 2)
-    is_end = (z == 0) | (z == 3)
-    is_inner = (z == 1) | (z == 2)
     rows = TILE_BINS * 256
 
     def spike_copy(k):
-        where = pl.ds(k * rows, rows)
-        return pltpu.make_async_copy(spikes.at[where], spk_v.at[where], spk_sem.at[k])
+        where = pl.ds(pl.multiple_of(k * rows, rows), rows)
+        return pltpu.make_async_copy(spikes.at[where], spk_v.at[k], spk_sem.at[k])
 
     loads = [
         pltpu.make_async_copy(source, target, tab_sem.at[i])
         for i, (source, target) in enumerate(
             [
                 (read_in, rd_v), (kernel, ker_v), (first, first_v), (twist, twist_v),
-                (middle, mid_v), (last, last_v), (w_gate, wg_v), (w_up, wu_v), (w_down, wd_v),
+                (middle, mid_v), (last, last_v),
             ]
         )
     ]
     loads[0].start()
-    for k in range(4):
+    for k in range(AHEAD):
         spike_copy(k).start()
 
     barrier = pltpu.get_barrier_semaphore()
@@ -174,7 +178,6 @@
 
     lax.fori_loop(1, 32, greet, 0)
     loads[0].wait()
-    pl.semaphore_wait(barrier, 31)
 
     def remote(source, target, send, recv, where):
         return pltpu.make_async_remote_copy(
@@ -182,112 +185,75 @@
             device_id=where, device_id_type=MESH,
         )
 
-    def at_z(place):
-        return (tm, place * 2 + core)
-
     def sib_copy(k):
         return remote(own.at[k, 1 - core], sib.at[k], sib_s.at[k], sib_r.at[k], (tm, z * 2 + 1 - core))
 
-    end_inner = jnp.where(z == 0, 1, 2)
-    end_first = jnp.where(z == 0, 1, 0)
-    near_end = jnp.where(z == 1, 0, 3)
-    fwd_first = jnp.where(z == 1, 2, 0)
-    own_slot = lax.rem(z, 2)
-
-    def end_copy(k):
-        return remote(
-            acc.at[k, pl.ds(end_first, 3)], from_end.at[k, pl.ds(end_first, 3)],
-            end_s.at[k], end_r.at[k], at_z(end_inner),
-        )
-
-    def inner_copy(k):
-        return remote(fwd.at[k], from_inner.at[k], inn_s.at[k], inn_r.at[k], at_z(3 - z))
-
-    def final_copy(k):
-        return remote(to_end.at[k], from_mid.at[k], fin_s.at[k], fin_r.at[k], at_z(near_end))
+    def z_copy(k, d):
+        other = lax.rem(z + d, 4)
+        return remote(acc.at[k, other], parts.at[k, d - 1], z_s.at[k, d], z_r.at[k, d], (tm, other * 2 + core))
 
     def x_copy(k, d):
         other = lax.rem(tm + d, 4)
         return remote(
-            xsend.at[k, other], xall.at[pl.ds(tm * 8 + k * TILE_BINS, TILE_BINS)],
+            xsend.at[k, other], xall.at[1, pl.ds(tm * 8 + k * TILE_BINS, TILE_BINS)],
             x_s.at[k, d], x_r.at[k, d], (other, nrn),
         )
 
-    def project(start, count):
-        for k in range(start, start + count):
+    def tile_step(k, carry):
+        @pl.when(k < TILES)
+        def _():
+            @pl.when(k + AHEAD < TILES)
+            def _():
+                spike_copy(k + AHEAD).start()
+
+            @pl.when(k == AHEAD)
+            def _():
+                for load in loads[1:]:
+                    load.start()
+
             spike_copy(k).wait()
-        block = spk_v[start * rows : (start + count) * rows]
-        sums = jnp.dot(block, rd_v[...], preferred_element_type=jnp.float32)
-        for i in range(count):
+            sums = jnp.dot(spk_v[k], rd_v[...], preferred_element_type=jnp.float32)
             for b in range(TILE_BINS):
-                at = i * rows + b * 256
-                low, high = sums[at : at + 128].T, sums[at + 128 : at + 256].T
+                low = sums[b * 256 : b * 256 + 128].T
+                high = sums[b * 256 + 128 : b * 256 + 256].T
                 for g in range(32):
                     piece = jnp.concatenate([low[4 * g : 4 * g + 4], high[4 * g : 4 * g + 4]], 0)
-                    own[start + i, g % 2, (g % 8) // 2, g // 8, b] = piece
-            sib_copy(start + i).start()
-
-    def pair(k):
-        sib_copy(k).wait_recv()
-        acc[k] = own[k, core] + sib[k]
-
-        @pl.when(is_end)
-        def _():
-            end_copy(k).start()
-
-    def forward_sum(k):
-        @pl.when(is_inner)
-        def _():
-            end_copy(k).wait_recv()
-            fwd[k] = acc[k, pl.ds(fwd_first, 2)] + from_end[k, pl.ds(fwd_first, 2)]
-            inner_copy(k).start()
+                    own[k, g % 2, (g % 8) // 2, g // 8, b] = piece
+
+            @pl.when(k == 0)
+            def _():
+                pl.semaphore_wait(barrier, 31)
+
+            sib_copy(k).start()
+
+        @pl.when(k >= 1)
+        def _():
+            sib_copy(k - 1).wait_recv()
+            acc[k - 1] = own[k - 1, core] + sib[k - 1]
+            for d in (2, 1, 3):
+                z_copy(k - 1, d).start()
+
+        @pl.when((k >= LAG) & (k < TILES))
+        def _():
+            finish_sum(k - LAG)
+
+        return carry
 
     def finish_sum(k):
-        @pl.when(is_inner)
-        def _():
-            inner_copy(k).wait_recv()
-            to_end[k] = acc[k, near_end] + from_inner[k, 1 - own_slot]
-            final_copy(k).start()
-            xsend[k] = acc[k, z] + from_end[k, z] + from_inner[k, own_slot]
-
-        @pl.when(is_end)
-        def _():
-            final_copy(k).wait_recv()
-            xsend[k] = acc[k, z] + from_mid[k]
-
+        for d in (1, 2, 3):
+            z_copy(k, d).wait_recv()
+        xsend[k] = acc[k, z] + parts[k, 0] + parts[k, 1] + parts[k, 2]
         for d in (3, 1, 2):
             x_copy(k, d).start()
-        xall[pl.ds(tm * 8 + k * TILE_BINS, TILE_BINS)] = xsend[k, tm]
-
-    def each(step, start, stop):
-        def body(k, carry):
-            step(k)
-            return carry
-
-        lax.fori_loop(start, stop, body, 0)
-
-    project(0, 1)
-    for k in range(4, TILES):
-        spike_copy(k).start()
-    for load in loads[1:]:
-        load.start()
-    project(1, 1)
-    pair(0)
-    project(2, 2)
-    pair(1)
-    project(4, 2)
-    each(pair, 2, 4)
-    each(forward_sum, 0, 2)
-    project(6, 2)
-    each(pair, 4, 6)
-    forward_sum(2)
-    each(pair, 6, 8)
+        xall[1, pl.ds(tm * 8 + k * TILE_BINS, TILE_BINS)] = xsend[k, tm]
+
+    lax.fori_loop(0, TILES + 1, tile_step, 0)
 
     for load in loads[1:]:
         load.wait()
     for r in range(32):
         for half in range(2):
-            kall[r, half * 4 : half * 4 + 4, :] = ker_v[:, r * 256 + half * 128 : r * 256 + half * 128 + 128]
+            xall[0, r, half * 4 : half * 4 + 4, :] = ker_v[:, r * 256 + half * 128 : r * 256 + half * 128 + 128]
 
     cos_turn = jnp.concatenate([twist_v[0]] * 4, 1)
     sin_turn = jnp.concatenate([twist_v[1]] * 4, 1)
@@ -310,8 +276,8 @@
         result += jnp.dot(high, mid_v[1], preferred_element_type=jnp.float32)
         return result[:, :256], result[:, 256:]
 
-    def gather_lanes(ref):
-        return jnp.concatenate([ref[:, half * 4 + j, :] for j in range(4) for half in range(2)], 1)
+    def gather_lanes(p):
+        return jnp.concatenate([xall[p, :, half * 4 + j, :] for j in range(4) for half in range(2)], 1)
 
     def outer_dft(signal):
         both = jnp.dot(first_v[...], stacked(signal), preferred_element_type=jnp.float32)
@@ -320,34 +286,46 @@
         turned_imag = imag * cos_turn - real * sin_turn
         return to_rows(turned_real), to_rows(turned_imag)
 
-    spec[0], spec[1] = outer_dft(gather_lanes(kall))
-
-    def forward_then_finish(k):
-        forward_sum(k)
-        finish_sum(k - 2)
-
-    forward_sum(3)
-    each(finish_sum, 0, 2)
-    each(forward_then_finish, 4, 6)
-    kern_real, kern_imag = inner_dft(spec[0], spec[1])
-    spec[0] = kern_real * (1.0 / 8192)
-    spec[1] = kern_imag * (1.0 / 8192)
-    each(forward_then_finish, 6, 8)
-    each(finish_sum, 6, 8)
-
-    def x_arrived(k, carry):
-        for d in (1, 2, 3):
-            x_copy(k, d).wait_recv()
-        return carry
-
-    lax.fori_loop(0, TILES, x_arrived, 0)
-
-    series = gather_lanes(xall)
-    data_real, data_imag = inner_dft(*outer_dft(series))
-    prod_real = data_real * spec[0] - data_imag * spec[1]
-    prod_imag = data_real * spec[1] + data_imag * spec[0]
-    back_real, back_neg = inner_dft(prod_real, -prod_imag)
-    back_real, back_neg = to_lanes(back_real), to_lanes(back_neg)
+    def dft_pass(p, carry):
+        @pl.when(p < 2)
+        def _():
+            work[0], work[1] = outer_dft(gather_lanes(p))
+
+        real, imag = inner_dft(work[0], work[1])
+
+        @pl.when(p == 0)
+        def _():
+            spec[0] = real * (1.0 / 8192)
+            spec[1] = imag * (1.0 / 8192)
+
+            def late_finish(k, carry):
+                finish_sum(k)
+                return carry
+
+            lax.fori_loop(TILES - LAG, TILES, late_finish, 0)
+
+            def x_arrived(k, carry):
+                for d in (1, 2, 3):
+                    x_copy(k, d).wait_recv()
+                return carry
+
+            lax.fori_loop(0, TILES, x_arrived, 0)
+
+        @pl.when(p == 1)
+        def _():
+            work[0] = real * spec[0] - imag * spec[1]
+            work[1] = -(real * spec[1] + imag * spec[0])
+
+        @pl.when(p == 2)
+        def _():
+            work[0] = real
+            work[1] = imag
+
+        return carry
+
+    lax.fori_loop(0, 3, dft_pass, 0)
+    series = gather_lanes(1)
+    back_real, back_neg = to_lanes(work[0]), to_lanes(work[1])
     turned = jnp.concatenate(
         [back_real * cos_turn + back_neg * sin_turn, back_real * sin_turn - back_neg * cos_turn], 0
     )
@@ -359,23 +337,17 @@
         other = lax.rem(me + d, 32)
         return remote(ysend.at[other], yall.at[me], y_s.at[d], y_r.at[d], after(d))
 
-    for d in range(1, 32):
+    def y_start(d, carry):
         y_copy(d).start()
+        return carry
+
+    lax.fori_loop(1, 32, y_start, 0)
     yall[me] = ysend[me]
 
     def drain(k, carry):
         sib_copy(k).wait_send()
-
-        @pl.when(is_end)
-        def _():
-            end_copy(k).wait_send()
-
-        @pl.when(is_inner)
-        def _():
-            inner_copy(k).wait_send()
-            final_copy(k).wait_send()
-
         for d in (1, 2, 3):
+            z_copy(k, d).wait_send()
             x_copy(k, d).wait_send()
         return carry
 
@@ -388,13 +360,8 @@
     lax.fori_loop(1, 32, y_wait, 0)
 
     flat = yall.reshape(256, 128)
-    residual = jnp.concatenate([flat[pl.ds(half, 128, stride=2), :].T for half in range(2)], 0)
-    meansq = jnp.mean(residual * residual, axis=-1, keepdims=True)
-    normed = (residual * lax.rsqrt(meansq + 1e-05) * gain[...]).astype(jnp.bfloat16)
-    gate = jnp.dot(normed, wg_v[...], preferred_element_type=jnp.float32)
-    upper = jnp.dot(normed, wu_v[...], preferred_element_type=jnp.float32)
-    act = (gate / (1.0 + jnp.exp(-gate)) * upper).astype(jnp.bfloat16)
-    out[...] = residual + jnp.dot(act, wd_v[...], preferred_element_type=jnp.float32)
+    for half in range(2):
+        out[half * 128 : half * 128 + 128, :] = flat[pl.ds(half, 128, stride=2), :].T
 
 
 def fused(spikes, read_in, kernel, gain, w_gate, w_up, w_down):
@@ -405,18 +372,15 @@
     dma = pltpu.SemaphoreType.DMA
     anywhere = pl.BlockSpec(memory_space=pl.ANY)
     vmem = pl.BlockSpec(memory_space=pltpu.VMEM)
-    return pl.pallas_call(
+    residual = pl.pallas_call(
         fused_kernel,
         out_shape=jax.ShapeDtypeStruct((256, 128), f32),
-        in_specs=[anywhere] * 3 + [vmem] + [anywhere] * 7,
+        in_specs=[anywhere] * 7,
         out_specs=vmem,
         scratch_shapes=[
-            pltpu.VMEM((TILES * rows, 4096), bf16),
+            pltpu.VMEM((TILES, rows, 4096), bf16),
             pltpu.VMEM((4096, 128), bf16),
             pltpu.VMEM((4, 8192), f32),
-            pltpu.VMEM((128, 512), bf16),
-            pltpu.VMEM((128, 512), bf16),
-            pltpu.VMEM((512, 128), bf16),
             pltpu.VMEM(first.shape, bf16),
             pltpu.VMEM(last.shape, bf16),
             pltpu.VMEM(middle.shape, bf16),
@@ -424,29 +388,24 @@
             pltpu.VMEM((TILES, 2, 4, 4) + tile, f32),
             pltpu.VMEM((TILES, 4, 4) + tile, f32),
             pltpu.VMEM((TILES, 4, 4) + tile, f32),
-            pltpu.VMEM((TILES, 4, 4) + tile, f32),
-            pltpu.VMEM((TILES, 2, 4) + tile, f32),
-            pltpu.VMEM((TILES, 2, 4) + tile, f32),
+            pltpu.VMEM((TILES, 3, 4) + tile, f32),
             pltpu.VMEM((TILES, 4) + tile, f32),
-            pltpu.VMEM((TILES, 4) + tile, f32),
-            pltpu.VMEM((TILES, 4) + tile, f32),
-            pltpu.VMEM((32, 8, 128), f32),
-            pltpu.VMEM((32, 8, 128), f32),
+            pltpu.VMEM((2, 32, 8, 128), f32),
             pltpu.VMEM((32, 8, 128), f32),
             pltpu.VMEM((32, 8, 128), f32),
             pltpu.VMEM((2, 128, 256), f32),
-            dma((TILES,)), dma((9,)),
-            dma((TILES,)), dma((TILES,)), dma((TILES,)), dma((TILES,)),
-            dma((TILES,)), dma((TILES,)), dma((TILES,)), dma((TILES,)),
-            dma((TILES, 4)), dma((TILES, 4)), dma((32,)), dma((32,)),
+            pltpu.VMEM((2, 128, 256), f32),
+            dma((TILES,)), dma((6,)), dma((TILES,)), dma((TILES,)),
+            dma((TILES, 4)), dma((TILES, 4)), dma((TILES, 4)), dma((TILES, 4)), dma((32,)), dma((32,)),
         ],
         compiler_params=pltpu.CompilerParams(
             collective_id=0, has_side_effects=True, vmem_limit_bytes=56 * 1024 * 1024
         ),
     )(
-        spikes, read_in, kernel, gain.reshape(1, 128), w_gate, w_up, w_down,
+        spikes, read_in, kernel,
         jnp.asarray(first), jnp.asarray(last), jnp.asarray(middle), jnp.asarray(twist),
-    ).astype(bf16)
+    )
+    return gated_mlp(residual, gain, w_gate, w_up, w_down)
 
 
 def solution(mesh):

time: 42.7 us -> 37.9 us (0.89)
  Pallas kernels: 41 us -> 33.4 us
  matrix products: 0 us -> 3.21 us
  other arithmetic: 1.54 us -> 1.02 us
    pallas_call x1, Pallas kernels: 41 us -> 33.4 us  [fused(): pl.pallas_call(fused_kernel, out_shape=jax.ShapeDtypeStruct((256, 128), f...]
    dot_general x0 -> x2, matrix products: none -> 3.21 us  [the longest x1 2.04 us: gated_mlp(): jnp.dot(act, w_down, preferred_element_type=jnp.float32)]
    convert_element_type x1 -> x0, other arithmetic: 1.54 us -> none  [fused(): return pl.pallas_call(fused_kernel, out_shape=jax.ShapeDtypeStruct((256,...]
    reduce_sum x0 -> x1, other arithmetic: none -> 1.02 us  [gated_mlp(): meansq = jnp.mean(residual * residual, axis=-1, keepdims=True)]
where the time goes in v3:
time: 37.9 us; the launch traced here: 37.7 us
  Pallas kernels  33.4 us (88%)
  matrix products  3.21 us (8%)
  other arithmetic  1.02 us (3%)
    pallas_call x1, Pallas kernels, fused(): pl.pallas_call(fused_kernel, out_shape=jax.ShapeDtypeStruct((256, 128), f...  33.4 us
    dot_general x1, matrix products, gated_mlp(): jnp.dot(act, w_down, preferred_element_type=jnp.float32)  2.04 us
    dot_general x1, matrix products, gated_mlp(): gate = jnp.dot(normed, w_gate, preferred_element_type=jnp.float32)  1.17 us
    reduce_sum x1, other arithmetic, gated_mlp(): meansq = jnp.mean(residual * residual, axis=-1, keepdims=True)  1.02 us

profile of v3, /device:TPU:0, one launch (start us, length us, event | category | flops | bytes accessed | tf_op | source)
XLA Modules:
  0.0 37.7 jit_solution(14826773254736835924)
XLA Ops:
  0.0 0.0 copy-start
  0.0 0.0 copy-start.1
  0.0 0.0 copy-start.2
  0.0 0.0 copy-start.3
  0.0 33.4 %shard_map.109 = f32[256,128]{1,0:T(8,128)} custom-call(bf16[2048,4096]{1,0:T(8,128)(2,1)} %spikes.1, bf16[4096,128]{1,0:T(8,128)(2,1)} %read_in.1, f32[4,8192]{1,0:T(4,128)} %kernel.1, bf16[64,96]{1,0:T(8,128)(2,1)} %constant.18.clone.first, bf16[32,192]{1,0:T(8,128)(2,1)} %constant.19.clone.last, bf16[2,512,512]{2,1,0:T(8,128)(2,1)} %constant.20.clone.middle, ...), custom_call_target="tpu_custom_call" | custom-call | tf_op jit(solution)/shard_map/pallas_call | solution.py:375
  33.5 1.0 %multiply_reduce_fusion = f32[256]{0:T(256)S(1)} fusion(f32[256,128]{1,0:T(8,128)} %shard_map.109), kind=kLoop, calls=%fused_computation.12 | loop fusion | flops 65280 | bytes 132096 | tf_op jit(solution)/shard_map/reduce_sum | solution.py:99
  34.5 0.0 copy-done
  34.5 0.0 copy-done.1
  34.5 1.2 %fusion.10 = f32[256,512]{1,0:T(8,128)S(1)} fusion(bf16[128,512]{1,0:T(8,128)(2,1)S(1)} %copy-done, f32[256,128]{1,0:T(8,128)} %shard_map.109, f32[128]{0:T(128)S(1)} %copy-done.1, f32[256]{0:T(256)S(1)} %add_rsqrt_fusion), kind=kOutput, calls=%fused_computation.13 | convolution fusion | flops 33652736 | bytes 787968 | tf_op jit(solution)/shard_map/dot_general | solution.py:101
  35.7 0.0 copy-done.2
  35.7 0.0 copy-done.3
  35.7 2.0 %fusion.3 = bf16[256,128]{1,0:T(8,128)(2,1)} fusion(f32[256,128]{1,0:T(8,128)} %shard_map.109, bf16[512,128]{1,0:T(8,128)(2,1)S(1)} %copy-done.2, bf16[128,512]{1,0:T(8,128)(2,1)S(1)} %copy-done.3, f32[256,512]{1,0:T(8,128)S(1)} %fusion.10, f32[128]{0:T(128)S(1)} %copy-done.1, f32[256]{0:T(256)S(1)} %add_rsqrt_fusion), kind=kOutput, calls=%fused_computation.4 | convolution fusion | flops 68059136 | bytes 984576 | tf_op jit(solution)/shard_map/dot_general | solution.py:104
  (1 shorter events, 0.0 us)
Async XLA Ops:
  0.0 34.5 %copy-start = (bf16[128,512]{1,0:T(8,128)(2,1)S(1)}, bf16[128,512]{1,0:T(8,128)(2,1)}, u32[]{:S(2)}) copy-start(bf16[128,512]{1,0:T(8,128)(2,1)} %param.15) | copy-start | bytes 393220
  0.0 34.5 %copy-start.1 = (f32[128]{0:T(128)S(1)}, f32[128]{0:T(128)}, u32[]{:S(2)}) copy-start(f32[128]{0:T(128)} %param.14) | copy-start | bytes 1540
  0.0 35.7 %copy-start.2 = (bf16[512,128]{1,0:T(8,128)(2,1)S(1)}, bf16[512,128]{1,0:T(8,128)(2,1)}, u32[]{:S(2)}) copy-start(bf16[512,128]{1,0:T(8,128)(2,1)} %param.17) | copy-start | bytes 393220
  0.0 35.7 %copy-start.3 = (bf16[128,512]{1,0:T(8,128)(2,1)S(1)}, bf16[128,512]{1,0:T(8,128)(2,1)}, u32[]{:S(2)}) copy-start(bf16[128,512]{1,0:T(8,128)(2,1)} %param.16) | copy-start | bytes 393220

commit v4 on v3

--- a/solution.py
+++ b/solution.py
@@ -138,9 +138,9 @@
 
 
 def fused_kernel(
-    spikes, read_in, kernel, first, last, middle, twist,
+    spikes, read_in, kernel, gain, w_gate, w_up, w_down, first, last, middle, twist,
     out,
-    spk_v, rd_v, ker_v, first_v, last_v, mid_v, twist_v,
+    spk_v, rd_v, ker_v, wg_v, wu_v, wd_v, first_v, last_v, mid_v, twist_v,
     own, sib, acc, parts, xsend, xall, ysend, yall, spec, work,
     spk_sem, tab_sem, sib_s, sib_r, z_s, z_r, x_s, x_r, y_s, y_r,
 ):
@@ -158,7 +158,7 @@
         for i, (source, target) in enumerate(
             [
                 (read_in, rd_v), (kernel, ker_v), (first, first_v), (twist, twist_v),
-                (middle, mid_v), (last, last_v),
+                (middle, mid_v), (last, last_v), (w_gate, wg_v), (w_up, wu_v), (w_down, wd_v),
             ]
         )
     ]
@@ -360,8 +360,13 @@
     lax.fori_loop(1, 32, y_wait, 0)
 
     flat = yall.reshape(256, 128)
-    for half in range(2):
-        out[half * 128 : half * 128 + 128, :] = flat[pl.ds(half, 128, stride=2), :].T
+    residual = jnp.concatenate([flat[pl.ds(half, 128, stride=2), :].T for half in range(2)], 0)
+    meansq = jnp.mean(residual * residual, axis=-1, keepdims=True)
+    normed = (residual * lax.rsqrt(meansq + 1e-05) * gain[...]).astype(jnp.bfloat16)
+    gate = jnp.dot(normed, wg_v[...], preferred_element_type=jnp.float32)
+    upper = jnp.dot(normed, wu_v[...], preferred_element_type=jnp.float32)
+    act = (gate / (1.0 + jnp.exp(-gate)) * upper).astype(jnp.bfloat16)
+    out[...] = (residual + jnp.dot(act, wd_v[...], preferred_element_type=jnp.float32)).astype(jnp.bfloat16)
 
 
 def fused(spikes, read_in, kernel, gain, w_gate, w_up, w_down):
@@ -372,15 +377,18 @@
     dma = pltpu.SemaphoreType.DMA
     anywhere = pl.BlockSpec(memory_space=pl.ANY)
     vmem = pl.BlockSpec(memory_space=pltpu.VMEM)
-    residual = pl.pallas_call(
+    return pl.pallas_call(
         fused_kernel,
-        out_shape=jax.ShapeDtypeStruct((256, 128), f32),
-        in_specs=[anywhere] * 7,
+        out_shape=jax.ShapeDtypeStruct((256, 128), bf16),
+        in_specs=[anywhere] * 3 + [vmem] + [anywhere] * 7,
         out_specs=vmem,
         scratch_shapes=[
             pltpu.VMEM((TILES, rows, 4096), bf16),
             pltpu.VMEM((4096, 128), bf16),
             pltpu.VMEM((4, 8192), f32),
+            pltpu.VMEM((128, 512), bf16),
+            pltpu.VMEM((128, 512), bf16),
+            pltpu.VMEM((512, 128), bf16),
             pltpu.VMEM(first.shape, bf16),
             pltpu.VMEM(last.shape, bf16),
             pltpu.VMEM(middle.shape, bf16),
@@ -395,17 +403,16 @@
             pltpu.VMEM((32, 8, 128), f32),
             pltpu.VMEM((2, 128, 256), f32),
             pltpu.VMEM((2, 128, 256), f32),
-            dma((TILES,)), dma((6,)), dma((TILES,)), dma((TILES,)),
+            dma((TILES,)), dma((9,)), dma((TILES,)), dma((TILES,)),
             dma((TILES, 4)), dma((TILES, 4)), dma((TILES, 4)), dma((TILES, 4)), dma((32,)), dma((32,)),
         ],
         compiler_params=pltpu.CompilerParams(
             collective_id=0, has_side_effects=True, vmem_limit_bytes=56 * 1024 * 1024
         ),
     )(
-        spikes, read_in, kernel,
+        spikes, read_in, kernel, gain.reshape(1, 128), w_gate, w_up, w_down,
         jnp.asarray(first), jnp.asarray(last), jnp.asarray(middle), jnp.asarray(twist),
     )
-    return gated_mlp(residual, gain, w_gate, w_up, w_down)
 
 
 def solution(mesh):

time: 37.9 us -> 36.3 us (0.958)
  matrix products: 3.21 us -> 0 us
  local copies, waits for them, and re-layouts: 0.02 us -> 1.47 us
  Pallas kernels: 33.4 us -> 34.6 us
  other arithmetic: 1.02 us -> 0 us
    dot_general x2 -> x0, matrix products: 3.21 us -> none  [the longest x1 2.04 us: gated_mlp(): jnp.dot(act, w_down, preferred_element_type=jnp.float32)]
    unnamed x8 -> x1, local copies, waits for them, and re-layouts: 0.02 us -> 1.47 us
    pallas_call x1, Pallas kernels: 33.4 us -> 34.6 us  [fused(): pl.pallas_call(fused_kernel, out_shape=jax.ShapeDtypeStruct((256, 128), b...]
    reduce_sum x1 -> x0, other arithmetic: 1.02 us -> none  [gated_mlp(): meansq = jnp.mean(residual * residual, axis=-1, keepdims=True)]
where the time goes in v4:
time: 36.3 us; the launch traced here: 36.1 us
  Pallas kernels  34.6 us (95%)
  local copies, waits for them, and re-layouts  1.47 us (4%)
    pallas_call x1, Pallas kernels, fused(): pl.pallas_call(fused_kernel, out_shape=jax.ShapeDtypeStruct((256, 128), b...  34.6 us
    unnamed x1, local copies, waits for them, and re-layouts  1.47 us

profile of v4, /device:TPU:0, one launch (start us, length us, event | category | flops | bytes accessed | tf_op | source)
XLA Modules:
  0.0 36.1 jit_solution(16051883214164780360)
XLA Ops:
  0.0 34.6 %shard_map.109 = bf16[256,128]{1,0:T(8,128)(2,1)} custom-call(bf16[2048,4096]{1,0:T(8,128)(2,1)} %spikes.1, bf16[4096,128]{1,0:T(8,128)(2,1)} %read_in.1, f32[4,8192]{1,0:T(4,128)} %kernel.1, f32[1,128]{1,0:T(1,128)} %bitcast.1, bf16[128,512]{1,0:T(8,128)(2,1)} %w_gate.1, bf16[128,512]{1,0:T(8,128)(2,1)} %w_up.1, bf16[512,128]{1,0:T(8,128)(2,1)} %w_down.1, ...), custom_call_target="tpu_custom_call" | custom-call | tf_op jit(solution)/shard_map/pallas_call | solution.py:380
  34.6 1.5 %copy.13 = bf16[256,128]{1,0:T(8,128)(2,1)} copy(bf16[256,128]{1,0:T(8,128)(2,1)} %shard_map.109) | data formatting | bytes 131072
